TPU v7x, 32 devices: a whole 2x2x4 slice. The times are simulated.
32 devices in a mesh: groups: 2 (over y), dp: 4 (over z), cent: 4 (over x, core).
Axes of the slice: x: 2, y: 2, z: 4, core: 2. Of those that a mesh axis runs over, the one named last changes fastest.
Arguments:
- rows: bfloat16 [2048, 1024], P(('groups', 'dp', 'cent')), parts along dimension 0, may hold values from -6 to 6
- coarse_ids: int32 [2048, 4], P(('groups', 'dp', 'cent')), parts along dimension 0, may hold values from 0 to 127, all different within a row; in each aligned block of 64 rows (0 to 63, 64 to 127, ...) at most 4 rows name the same one
- parent: int32 [65536], P('groups'), parts along dimension 0, may hold values from 0 to 127, as said below
- fine_cent: bfloat16 [65536, 1024], P(('groups', 'dp', 'cent')), parts along dimension 0, may hold values from -16 to 16
- coarse_cent: bfloat16 [256, 1024], P('groups'), parts along dimension 0, may hold values from -16 to 16
Outputs:
- fine_out: bfloat16 [65536, 1024], P(('groups', 'dp', 'cent')), parts along dimension 0
- coarse_out: bfloat16 [256, 1024], P('groups'), parts along dimension 0
There are 2 independent parts, one for each index of `groups`. A program takes and returns all parts, laid end to end along the dimension named above; each array names one. Nothing has to cross between parts.
Inputs may be any that keep to these rules, and one draw needn't show every extreme that they name: `coarse_ids`: in each aligned block of 64 rows (the rows of one device) no coarse cluster is named by more than 4 rows, and the ids of one row differ. `parent`: each coarse cluster has exactly 256 children; the fine clusters form 4 * 4 blocks of consecutive indices of equal size, and each block holds all the children of its coarse clusters.
All inputs are finite; a program needn't handle non-finite values.
Results may differ from a plain program's by a relative error of at most 0.0048.
Values may be sent and summed in bfloat16 or wider, within the bound.
A program may use at most 64 MiB of HBM per device.

v0:
```python
import math

import jax
import jax.numpy as jnp
from jax import lax
from jax.sharding import PartitionSpec as P

COARSE = 128
TOP = 4
ITERS = 2
MOST = 4


def route_tables(parent, owners):
    cluster_ids = jnp.arange(COARSE, dtype=jnp.int32)
    blocks = parent.reshape(owners, -1)
    present = jnp.any(blocks[:, :, None] == cluster_ids[None, None, :], axis=1)
    owner_ids = jnp.arange(owners, dtype=jnp.int32)[:, None]
    owner = jnp.sum(jnp.where(present, owner_ids, 0), axis=0)
    same = owner[:, None] == owner[None, :]
    below = cluster_ids[None, :] < cluster_ids[:, None]
    local = jnp.sum((same & below).astype(jnp.int32), axis=1)
    return (owner, local)


def pair_slots(block_ids, position):
    flat = block_ids.reshape(-1)
    count = flat.shape[0]
    hits = flat[:, None] == jnp.arange(COARSE, dtype=jnp.int32)[None, :]
    onehot = hits.astype(jnp.float32)
    earlier = (
        jnp.arange(count, dtype=jnp.int32)[None, :] < jnp.arange(count, dtype=jnp.int32)[:, None]
    ).astype(jnp.float32)
    before = jnp.dot(
        earlier, onehot, preferred_element_type=jnp.float32, precision=lax.Precision.HIGHEST
    )
    rank = jnp.sum(before * onehot, axis=1).astype(jnp.int32)
    base = jnp.sum(jnp.where(hits, position[None, :], 0), axis=1)
    return base * MOST + rank


def coarse_weights(rows, match, coarse):
    scale = 1.0 / math.sqrt(rows.shape[1])
    coarse_f = coarse.astype(jnp.float32)
    norms = jnp.sum(coarse_f * coarse_f, axis=1)
    dots = lax.dot_general(
        rows, coarse, (((1,), (1,)), ((), ())), preferred_element_type=jnp.float32
    )
    full = (dots - 0.5 * norms[None, :]) * scale
    picked = jnp.sum(full[:, None, :] * match, axis=2)
    return jax.nn.softmax(picked, axis=1)


def owner_update(arrived, arrived_q, centroids, slot_group, fine_group):
    scale = 1.0 / math.sqrt(arrived.shape[-1])
    cent_f = centroids.astype(jnp.float32)
    norms = jnp.sum(cent_f * cent_f, axis=-1)
    dots = lax.dot_general(
        arrived, centroids, (((1,), (1,)), ((), ())), preferred_element_type=jnp.float32
    )
    logits = (dots - 0.5 * norms[None, :]) * scale
    allowed = slot_group[:, None] == fine_group[None, :]
    prob = jax.nn.softmax(jnp.where(allowed, logits, -jnp.inf), axis=-1)
    resp = arrived_q.astype(jnp.float32)[:, None] * prob
    resp_b = resp.astype(jnp.bfloat16)
    fine_sum = lax.dot_general(
        resp_b, arrived, (((0,), (0,)), ((), ())), preferred_element_type=jnp.float32
    )
    mass = jnp.sum(resp, axis=0)
    return ((fine_sum + cent_f) / (mass[:, None] + 1.0)).astype(jnp.bfloat16)


def send_both(outgoing, outgoing_q):
    return (
        lax.all_to_all(outgoing, ("dp", "cent"), split_axis=0, concat_axis=0, tiled=True),
        lax.all_to_all(outgoing_q, ("dp", "cent"), split_axis=0, concat_axis=0, tiled=True),
    )


def send_weights(outgoing_q):
    return lax.all_to_all(outgoing_q, ("dp", "cent"), split_axis=0, concat_axis=0, tiled=True)


def on_device(rows, coarse_ids, parent, fine_cent, coarse_cent):
    n_outer = lax.axis_size("dp")
    n_inner = lax.axis_size("cent")
    owners = n_outer * n_inner
    myself = lax.axis_index("dp") * n_inner + lax.axis_index("cent")
    block_size = fine_cent.shape[0]
    width_d = fine_cent.shape[1]
    row_count = rows.shape[0]
    per_owner = COARSE // owners
    width = per_owner * MOST
    slot_total = COARSE * MOST
    cluster_ids = jnp.arange(COARSE, dtype=jnp.int32)
    owner, local = route_tables(parent, owners)
    position = owner * per_owner + local
    slots = pair_slots(coarse_ids, position)
    slot_hits = slots[:, None] == jnp.arange(slot_total, dtype=jnp.int32)[None, :]
    slot_hits_b = slot_hits.astype(jnp.bfloat16)
    select = jnp.any(slot_hits.reshape(row_count, TOP, slot_total), axis=1).astype(jnp.bfloat16)
    outgoing = (
        lax.dot_general(select, rows, (((0,), (0,)), ((), ())), preferred_element_type=jnp.float32)
        .astype(jnp.bfloat16)
        .reshape(owners, width, width_d)
    )
    match = (coarse_ids[:, :, None] == cluster_ids[None, None, :]).astype(jnp.float32)
    mine = lax.dynamic_slice_in_dim(parent, myself * block_size, block_size)
    fine_group = jnp.sum(
        jnp.where(mine[:, None] == cluster_ids[None, :], local[None, :], 0), axis=1
    )
    slot_group = jnp.arange(owners * width, dtype=jnp.int32) % width // MOST
    placement = (position[:, None] == cluster_ids[None, :]).astype(jnp.bfloat16)
    prior = float(max(1, row_count * owners // COARSE))
    coarse = coarse_cent
    centroids = fine_cent
    arrived = outgoing
    for turn in range(ITERS):
        weights = coarse_weights(rows, match, coarse)
        pair_q = weights.astype(jnp.bfloat16).reshape(-1)
        outgoing_q = (
            lax.dot_general(
                pair_q, slot_hits_b, (((0,), (0,)), ((), ())), preferred_element_type=jnp.float32
            )
            .astype(jnp.bfloat16)
            .reshape(owners, width)
        )
        if turn == 0:
            arrived, arrived_q = send_both(outgoing, outgoing_q)
        else:
            arrived_q = send_weights(outgoing_q)
        blocks_in = arrived.reshape(owners, per_owner, MOST, width_d)
        q_in = arrived_q.reshape(owners, per_owner, MOST)
        owned_total = jnp.einsum(
            "slm,slmd->ld", q_in, blocks_in, preferred_element_type=jnp.float32
        )
        owned_mass = jnp.sum(q_in.astype(jnp.float32), axis=(0, 2))
        placed = lax.dot_general(
            placement, coarse, (((0,), (0,)), ((), ())), preferred_element_type=jnp.float32
        ).astype(jnp.bfloat16)
        own_rows = lax.dynamic_slice_in_dim(placed, myself * per_owner, per_owner, 0)
        updated = (
            (owned_total + prior * own_rows.astype(jnp.float32)) / (owned_mass[:, None] + prior)
        ).astype(jnp.bfloat16)
        collected = lax.all_gather(updated, ("dp", "cent"), axis=0, tiled=True)
        new_coarse = jnp.dot(placement, collected, preferred_element_type=jnp.float32).astype(
            jnp.bfloat16
        )
        centroids = owner_update(
            arrived.reshape(owners * width, width_d),
            arrived_q.reshape(-1),
            centroids,
            slot_group,
            fine_group,
        )
        coarse = new_coarse
    return (centroids, coarse)


def solution(mesh):
    in_specs = (
        P(("groups", "dp", "cent"), None),
        P(("groups", "dp", "cent"), None),
        P("groups"),
        P(("groups", "dp", "cent"), None),
        P("groups", None),
    )
    out_specs = (P(("groups", "dp", "cent"), None), P("groups", None))
    return jax.shard_map(
        on_device, mesh=mesh, in_specs=in_specs, out_specs=out_specs, check_vma=False
    )
```

profile of v0, /device:TPU:0, one launch (start us, length us, event | category | flops | bytes accessed | tf_op | source)
XLA Modules:
  0.0 139.9 jit_solution(14348013065673380173)
XLA Ops:
  0.6 1.1 multiply_reduce_fusion.1
  1.8 0.8 copy.28
  2.5 1.2 fusion.14
  3.7 0.9 select_reduce_fusion.3
  5.2 0.9 eq.62
  6.2 5.7 %fusion = pred[16,128]{1,0:T(8,128)(4,1)S(1)} fusion(s32[16,2048]{1,0:T(8,128)S(1)} %eq.62), kind=kLoop, calls=%fused_computation.1 | loop fusion | flops 8386560 | bytes 133120 | tf_op jit(solution)/shard_map/reduce_or | solution.py:17
  12.5 0.7 all_to_all.20
  13.2 7.4 %all-to-all-start = ((bf16[16,1,32]{2,1,0:T(2,128)(2,1)}), bf16[16,1,32]{2,1,0:T(2,128)(2,1)S(1)}, u32[]{:S(2)}, u32[]{:S(2)}) async-start(bf16[16,1,32]{2,1,0:T(2,128)(2,1)} %all_to_all.20), calls=%async_computation | async-start | bytes 16384 | tf_op jit(solution)/shard_map/all_to_all | solution.py:76
  20.9 1.5 %convolution_convert_fusion = bf16[512,1024]{1,0:T(8,128)(2,1)} fusion(pred[64,512]{1,0:T(8,128)(4,1)S(1)} %fusion.17, bf16[64,1024]{1,0:T(8,128)(2,1)S(1)} %copy-done), kind=kOutput, calls=%fused_computation.22 | convolution fusion | flops 67633152 | bytes 1212416 | tf_op jit(solution)/shard_map/dot_general | solution.py:103
  22.3 4.5 %all-to-all-done = bf16[16,1,32]{2,1,0:T(2,128)(2,1)S(1)} async-done(((bf16[16,1,32]{2,1,0:T(2,128)(2,1)}), bf16[16,1,32]{2,1,0:T(2,128)(2,1)S(1)}, u32[]{:S(2)}, u32[]{:S(2)}) %all-to-all-start) | async-done | bytes 1056 | tf_op jit(solution)/shard_map/all_to_all | solution.py:76
  26.9 3.7 %all-to-all-start.1 = ((bf16[16,32,1024]{2,1,0:T(8,128)(2,1)}), bf16[16,32,1024]{2,1,0:T(8,128)(2,1)S(1)}, u32[]{:S(2)}, u32[]{:S(2)}) async-start(bf16[16,32,1024]{2,1,0:T(8,128)(2,1)} %bitcast.3), calls=%async_computation.1 | async-start | bytes 2097152 | tf_op jit(solution)/shard_map/all_to_all | solution.py:75
  30.5 6.4 %copy.34 = bf16[2048,1024]{0,1:T(8,128)(2,1)} copy(bf16[2048,1024]{1,0:T(8,128)(2,1)} %param.8) | data formatting | bytes 8388608 | tf_op args[3]
  37.0 0.6 select_reduce_fusion
  37.6 3.1 %fusion.1 = f32[2048]{0:T(1024)S(1)} fusion(bf16[2048,1024]{0,1:T(8,128)(2,1)} %copy.34), kind=kLoop, calls=%fused_computation.6 | loop fusion | flops 6289408 | bytes 4202496 | tf_op jit(solution)/shard_map/reduce_sum | solution.py:57
  41.5 11.9 %all-to-all-done.1 = bf16[16,32,1024]{2,1,0:T(8,128)(2,1)S(1)} async-done(((bf16[16,32,1024]{2,1,0:T(8,128)(2,1)}), bf16[16,32,1024]{2,1,0:T(8,128)(2,1)S(1)}, u32[]{:S(2)}, u32[]{:S(2)}) %all-to-all-start.1) | async-done | bytes 1048608 | tf_op jit(solution)/shard_map/all_to_all | solution.py:75
  53.4 0.6 copy.44
  54.4 23.2 %all_gather.6 = bf16[128,1024]{1,0:T(8,128)(2,1)S(1)} all-gather(bf16[8,1024]{1,0:T(8,128)(2,1)S(1)} %fusion.27), channel_id=1, replica_groups=mesh['groups'=2,'dp'=4,'cent'=4] {'dp','cent'}, dimensions={0}, use_global_device_ids=true | all-gather | bytes 278528 | tf_op jit(solution)/shard_map/all_gather | solution.py:145
  77.6 0.3 multiply_reduce_fusion
  79.0 0.7 all_to_all.21
  79.6 3.7 %all-to-all-start.2 = ((bf16[16,1,32]{2,1,0:T(2,128)(2,1)}), bf16[16,1,32]{2,1,0:T(2,128)(2,1)S(1)}, u32[]{:S(2)}, u32[]{:S(2)}) async-start(bf16[16,1,32]{2,1,0:T(2,128)(2,1)} %all_to_all.21), calls=%async_computation.2 | async-start | bytes 16384 | tf_op jit(solution)/shard_map/all_to_all | solution.py:81
  83.3 4.8 %fusion.46 = (f32[512]{0:T(512)S(1)}, f32[512,2048]{1,0:T(8,128)S(1)}) fusion(f32[2048]{0:T(1024)S(1)} %broadcast_multiply_fusion.1, bf16[512,1024]{1,0:T(8,128)(2,1)S(1)} %bitcast.47, bf16[2048,1024]{1,0:T(8,128)(2,1)} %param.8, s32[2048]{0:T(1024)S(1)} %select_reduce_fusion, s32[512]{0:T(512)S(1)} %add_select_fusion), kind=kOutput, calls=%fused_computation.108 | convolution fusion | flops 2152726016 | bytes 9457664 | tf_op jit(solution)/shard_map/dot_general | solution.py:58
  88.1 0.7 fusion.7
  88.8 1.1 fusion.44
  90.3 3.8 %fusion.4 = (f32[2048]{0:T(1024)S(1)}, bf16[2048,1024]{0,1:T(8,128)(2,1)S(1)}) fusion(f32[2048]{0:T(1024)S(1)} %broadcast_add_fusion.1, bf16[2048,1024]{0,1:T(8,128)(2,1)S(1)} %copy-done.1, bf16[512,1024]{1,0:T(8,128)(2,1)S(1)} %bitcast.48, f32[512]{0:T(512)S(1)} %fusion.7, f32[512,2048]{1,0:T(8,128)S(1)} %get-tuple-element.15, ...), kind=kOutput, calls=%fused_computation.9 | convolution fusion | flops 2166355968 | bytes 13654016 | tf_op jit(solution)/shard_map/dot_general | solution.py:66
  94.2 2.7 %fusion.47 = (f32[512]{0:T(512)S(1)}, f32[512,2048]{1,0:T(8,128)S(1)}) fusion(f32[2048]{0:T(1024)S(1)} %broadcast_multiply_fusion, bf16[512,1024]{1,0:T(8,128)(2,1)S(1)} %bitcast.49, bf16[2048,1024]{0,1:T(8,128)(2,1)S(1)} %get-tuple-element.17, s32[2048]{0:T(1024)S(1)} %select_reduce_fusion, s32[512]{0:T(512)S(1)} %add_select_fusion), kind=kOutput, calls=%fused_computation.109 | convolution fusion | flops 2152726016 | bytes 9457664 | tf_op jit(solution)/shard_map/dot_general | solution.py:58
  96.9 1.9 %copy-done.2 = f32[512,2048]{1,0:T(8,128)} copy-done((f32[512,2048]{1,0:T(8,128)}, f32[512,2048]{1,0:T(8,128)S(1)}, u32[]{:S(2)}) %copy-start.2) | copy-done | bytes 4194328
  98.8 0.7 fusion.8
  100.7 22.5 %all_gather.7 = bf16[128,1024]{1,0:T(8,128)(2,1)S(1)} all-gather(bf16[8,1024]{1,0:T(8,128)(2,1)S(1)} %fusion.25), channel_id=1, replica_groups=mesh['groups'=2,'dp'=4,'cent'=4] {'dp','cent'}, dimensions={0}, use_global_device_ids=true | all-gather | bytes 278528 | tf_op jit(solution)/shard_map/all_gather | solution.py:145
  123.3 1.0 convolution_convert_fusion.1
  124.3 3.1 %fusion.45 = f32[2048]{0:T(1024)S(1)} fusion(f32[512]{0:T(512)S(1)} %fusion.8, f32[512,2048]{1,0:T(8,128)} %copy-done.2, f32[512]{0:T(512)S(1)} %get-tuple-element.18, f32[512]{0:T(512)S(1)} %reshape.182), kind=kLoop, calls=%fused_computation.107 | loop fusion | flops 4192256 | bytes 4208640 | tf_op jit(solution)/shard_map/reduce_sum | solution.py:69
  127.4 6.1 %fusion.6 = bf16[2048,1024]{0,1:T(8,128)(2,1)} fusion(bf16[2048,1024]{0,1:T(8,128)(2,1)} %copy-done.6, f32[2048]{0:T(1024)S(1)} %broadcast_add_fusion, bf16[512,1024]{1,0:T(8,128)(2,1)S(1)} %bitcast.50, f32[512,2048]{1,0:T(8,128)S(1)} %copy-done.3, f32[512]{0:T(512)S(1)} %fusion.8, f32[512]{0:T(512)S(1)} %get-tuple-element.18, f32[512]{0:T(512)S(1)} %reshape.182), kind=kOutput, calls=%fused_computation.11 | convolution fusion | flops 2160066560 | bytes 13645824 | tf_op jit(solution)/shard_map/dot_general | solution.py:66
  133.5 6.4 %copy.37 = bf16[2048,1024]{1,0:T(8,128)(2,1)} copy(bf16[2048,1024]{0,1:T(8,128)(2,1)} %fusion.6) | data formatting | bytes 8388608
  (67 shorter events, 5.2 us)
Async XLA Ops:
  0.6 1.9 %copy-start = (bf16[64,1024]{1,0:T(8,128)(2,1)S(1)}, bf16[64,1024]{1,0:T(8,128)(2,1)}, u32[]{:S(2)}) copy-start(bf16[64,1024]{1,0:T(8,128)(2,1)} %param.5) | copy-start | bytes 393220
  13.2 13.7 %all-to-all-start = ((bf16[16,1,32]{2,1,0:T(2,128)(2,1)}), bf16[16,1,32]{2,1,0:T(2,128)(2,1)S(1)}, u32[]{:S(2)}, u32[]{:S(2)}) async-start(bf16[16,1,32]{2,1,0:T(2,128)(2,1)} %all_to_all.20), calls=%async_computation | async-start | bytes 16384 | tf_op jit(solution)/shard_map/all_to_all | solution.py:76
  26.9 26.6 %all-to-all-start.1 = ((bf16[16,32,1024]{2,1,0:T(8,128)(2,1)}), bf16[16,32,1024]{2,1,0:T(8,128)(2,1)S(1)}, u32[]{:S(2)}, u32[]{:S(2)}) async-start(bf16[16,32,1024]{2,1,0:T(8,128)(2,1)} %bitcast.3), calls=%async_computation.1 | async-start | bytes 2097152 | tf_op jit(solution)/shard_map/all_to_all | solution.py:75
  30.5 6.5 %dynamic-slice-start = ((s32[32768]{0:T(1024)}, s32[]{:T(128)}), s32[2048]{0:T(1024)S(1)}, s32[]{:S(2)}) async-start(s32[32768]{0:T(1024)} %param.7, s32[]{:T(128)} %select_n.51), calls=%async_computation.3 | async-start | bytes 16896 | tf_op jit(solution)/shard_map/dynamic_slice | solution.py:108
  37.0 3.7 %copy-start.4 = (bf16[128,1024]{1,0:T(8,128)(2,1)S(1)}, bf16[128,1024]{1,0:T(8,128)(2,1)}, u32[]{:S(2)}) copy-start(bf16[128,1024]{1,0:T(8,128)(2,1)} %param.9) | copy-start | bytes 786436
  37.6 40.6 %copy-start.5 = (s32[64,4]{0,1:T(4,128)S(1)}, s32[64,4]{0,1:T(4,128)}, u32[]{:S(2)}) copy-start(s32[64,4]{0,1:T(4,128)} %param.6) | copy-start | bytes 3076
  79.6 20.2 %all-to-all-start.2 = ((bf16[16,1,32]{2,1,0:T(2,128)(2,1)}), bf16[16,1,32]{2,1,0:T(2,128)(2,1)S(1)}, u32[]{:S(2)}, u32[]{:S(2)}) async-start(bf16[16,1,32]{2,1,0:T(2,128)(2,1)} %all_to_all.21), calls=%async_computation.2 | async-start | bytes 16384 | tf_op jit(solution)/shard_map/all_to_all | solution.py:81
  88.1 2.2 %copy-start.1 = (bf16[2048,1024]{0,1:T(8,128)(2,1)S(1)}, bf16[2048,1024]{0,1:T(8,128)(2,1)}, u32[]{:S(2)}) copy-start(bf16[2048,1024]{0,1:T(8,128)(2,1)} %copy.34) | copy-start | bytes 12582916
  94.2 2.8 %copy-start.6 = (bf16[2048,1024]{0,1:T(8,128)(2,1)}, bf16[2048,1024]{0,1:T(8,128)(2,1)S(1)}, u32[]{:S(2)}) copy-start(bf16[2048,1024]{0,1:T(8,128)(2,1)S(1)} %get-tuple-element.17) | copy-start | bytes 12582916
  96.9 1.9 %copy-start.2 = (f32[512,2048]{1,0:T(8,128)}, f32[512,2048]{1,0:T(8,128)S(1)}, u32[]{:S(2)}) copy-start(f32[512,2048]{1,0:T(8,128)S(1)} %get-tuple-element.19) | copy-start | bytes 12582916
  100.6 26.8 %copy-start.3 = (f32[512,2048]{1,0:T(8,128)S(1)}, f32[512,2048]{1,0:T(8,128)}, u32[]{:S(2)}) copy-start(f32[512,2048]{1,0:T(8,128)} %copy-done.2) | copy-start | bytes 12582916
where the time goes:
time: 141 us; the launch traced here: 140 us
  blocking collectives  45.8 us (32%)
  matrix products  23.8 us (17%)
  local copies, waits for them, and re-layouts  20 us (14%)
  other arithmetic  18.3 us (13%)
  waiting for transfers between devices  16.4 us (12%)
  starting transfers between devices  14.7 us (10%)
    all_gather x2, blocking collectives, on_device(): collected = lax.all_gather(updated, ('dp', 'cent'), axis=0, tiled=True)  45.8 us
    unnamed x17, local copies, waits for them, and re-layouts  15.9 us
    all_to_all x1, waiting for transfers between devices, send_both(): lax.all_to_all(outgoing, ('dp', 'cent'), split_axis=0, concat_axis=0, til...  11.9 us
    dot_general x2, matrix products, owner_update(): lax.dot_general(resp_b, arrived, (((0,), (0,)), ((), ())), preferred_elem...  9.97 us
    dot_general x2, matrix products, owner_update(): lax.dot_general(arrived, centroids, (((1,), (1,)), ((), ())), preferred_e...  7.54 us
    all_to_all x1, starting transfers between devices, send_both(): lax.all_to_all(outgoing_q, ('dp', 'cent'), split_axis=0, concat_axis=0, t...  7.36 us
    reduce_or x1, other arithmetic, route_tables(): present = jnp.any(blocks[:, :, None] == cluster_ids[None, None, :], axis=1)  5.69 us
    all_to_all x1, waiting for transfers between devices, send_both(): lax.all_to_all(outgoing_q, ('dp', 'cent'), split_axis=0, concat_axis=0, t...  4.51 us
  transfers between devices with their start and end apart: 3, of which 2 were waited for; matrix products, arithmetic and copies ran while one was open for 19% of the time, Pallas kernels for 0%

commit v1 on v0

v1 whole, which is shorter than its diff:
```python
import functools
import math

import jax
import jax.numpy as jnp
from jax import lax
from jax.experimental import pallas as pl
from jax.experimental.pallas import tpu as pltpu
from jax.sharding import PartitionSpec as P

ITERS = 2
MOST = 4
BF = jnp.bfloat16
F32 = jnp.float32
NT = (((1,), (1,)), ((), ()))
TN = (((0,), (0,)), ((), ()))


def gather_kernel(nz, nc, rows_ref, ids_ref, rows_all, ids_all, rsend, rrecv, isend, irecv, local_sem):
    nx = nc // 2
    g = lax.axis_index("groups")
    z = lax.axis_index("dp")
    ce = lax.axis_index("cent")
    x = ce // 2
    core = ce % 2
    other = x * 2 + (1 - core)
    here = lambda zz, cc: (g, zz, cc)

    barrier = pltpu.get_barrier_semaphore()
    links = [
        (z > 0, here(z - 1, ce)),
        (z < nz - 1, here(z + 1, ce)),
        (x > 0, here(z, ce - 2)),
        (x < nx - 1, here(z, ce + 2)),
    ]
    for ok, dev in links:
        @pl.when(ok)
        def _():
            pl.semaphore_signal(barrier, inc=1, device_id=dev, device_id_type=pl.DeviceIdType.MESH)
    pl.semaphore_signal(
        barrier, inc=1, device_id=here(z, other), device_id_type=pl.DeviceIdType.MESH
    )
    mine = pltpu.make_async_copy(rows_ref, rows_all.at[z, ce], local_sem)
    mine.start()
    ids_all[z, ce] = ids_ref[...]
    degree = 1 + sum(ok.astype(jnp.int32) for ok, _ in links)
    mine.wait()
    pl.semaphore_wait(barrier, degree)

    def copies(zc, cc, way, dev):
        out = []
        for buf, ss, rs in ((rows_all, rsend, rrecv), (ids_all, isend, irecv)):
            out.append(
                pltpu.make_async_remote_copy(
                    src_ref=buf.at[zc, cc],
                    dst_ref=buf.at[zc, cc],
                    send_sem=ss.at[way, zc, cc],
                    recv_sem=rs.at[zc, cc],
                    device_id=dev,
                    device_id_type=pl.DeviceIdType.MESH,
                )
            )
        return out

    def send(zc, cc, way, dev, ok=None):
        def go():
            for c in copies(zc, cc, way, dev):
                c.start()
        if ok is None:
            go()
        else:
            pl.when(ok)(go)

    def wait_in(zc, cc):
        for c in copies(zc, cc, 0, here(z, other)):
            c.wait_recv()

    def on_x(zc, xc, right, left):
        cc = xc * 2 + core
        send(zc, cc, 3, here(z, ce + 2), right & (x < nx - 1))
        send(zc, cc, 2, here(z, ce - 2), left & (x > 0))
        send(zc, cc, 4, here(z, other))

    true = z >= 0

    def z_chunk(zc, up, down):
        send(zc, ce, 1, here(z + 1, ce), up & (z < nz - 1))
        send(zc, ce, 0, here(z - 1, ce), down & (z > 0))
        on_x(zc, x, true, true)

    def each_z(d, fn):
        if d == 0:
            fn(z, 0)
            return
        for sign in (-1, 1):
            zc = z + sign * d
            @pl.when((zc >= 0) & (zc < nz))
            def _():
                fn(zc, sign)

    def z_step(zc, sign):
        if sign == 0:
            z_chunk(zc, true, true)
        else:
            wait_in(zc, ce)
            z_chunk(zc, true if sign < 0 else ~true, true if sign > 0 else ~true)

    for t in range(nz + nx - 1):
        if t < nz:
            each_z(t, z_step)
        for e in range(1, nx):
            d = t - e
            if d < 0 or d >= nz:
                continue
            for sign in (-1, 1):
                xc = x + sign * e
                @pl.when((xc >= 0) & (xc < nx))
                def _():
                    def one(zc, _):
                        wait_in(zc, xc * 2 + core)
                        on_x(zc, xc, true if sign < 0 else ~true, true if sign > 0 else ~true)
                    each_z(d, one)

    for t in range(nz):
        def one(zc, _):
            for xc in range(nx):
                wait_in(zc, xc * 2 + (1 - core))
        each_z(t, one)
    def sent(zc, cc, way, ok):
        @pl.when(ok)
        def _():
            for c in copies(zc, cc, way, here(z, other)):
                c.wait_send()
    for zc in range(nz):
        sent(zc, ce, 1, (zc <= z) & (z < nz - 1))
        sent(zc, ce, 0, (zc >= z) & (z > 0))
        for xc in range(nx):
            cc = xc * 2 + core
            sent(zc, cc, 3, (xc <= x) & (x < nx - 1))
            sent(zc, cc, 2, (xc >= x) & (x > 0))
            sent(zc, cc, 4, true)


def gather(nz, nc, rows, ids):
    count, width = rows.shape
    return pl.pallas_call(
        functools.partial(gather_kernel, nz, nc),
        out_shape=(
            jax.ShapeDtypeStruct((nz, nc, count, width), BF),
            jax.ShapeDtypeStruct((nz, nc) + ids.shape, jnp.int32),
        ),
        in_specs=[pl.BlockSpec(memory_space=pltpu.VMEM)] * 2,
        out_specs=(pl.BlockSpec(memory_space=pltpu.VMEM),) * 2,
        scratch_shapes=[
            pltpu.SemaphoreType.DMA((5, nz, nc)),
            pltpu.SemaphoreType.DMA((nz, nc)),
            pltpu.SemaphoreType.DMA((5, nz, nc)),
            pltpu.SemaphoreType.DMA((nz, nc)),
            pltpu.SemaphoreType.DMA,
        ],
        compiler_params=pltpu.CompilerParams(
            collective_id=0, has_side_effects=True, vmem_limit_bytes=40 * 2**20
        ),
    )(rows, ids)


def iota(shape, dim):
    return lax.broadcasted_iota(jnp.int32, shape, dim)


def update_kernel(
    senders, per_sender, owned, rows_ref, ids_ref, parent_ref, fine_ref, coarse_ref,
    fine_out, coarse_out, match, mrank, qbuf, arrived, logit, cent, parent_col, sel,
):
    total, width = rows_ref.shape
    coarse_n = coarse_ref.shape[0]
    block = fine_ref.shape[0]
    slot_w = owned * MOST
    slots = senders * slot_w
    scale = 1.0 / math.sqrt(width)
    log2e = math.log2(math.e)
    prior = float(max(1, total // coarse_n))
    per_group = max(1, 128 // slot_w)
    group_rows = per_group * per_sender
    group_slots = per_group * slot_w
    groups = senders // per_group
    tile = min(512, block)
    tiles = block // tile

    nz_rows = block // 128
    me = lax.axis_index("dp") * lax.axis_size("cent") + lax.axis_index("cent")
    own = parent_ref[pl.ds(pl.multiple_of(me * nz_rows, nz_rows), nz_rows), :]
    if nz_rows < 8:
        own = jnp.concatenate([own] * (8 // nz_rows), axis=0)
    own_t = jnp.transpose(own.astype(F32))
    present = jnp.zeros((128, coarse_n), jnp.bool_)
    lanes = iota((128, coarse_n), 1)
    for b in range(nz_rows):
        col = own_t[:, b : b + 1].astype(jnp.int32)
        parent_col[pl.ds(b * 128, 128), :] = jnp.broadcast_to(col, (128, 128))
        present = present | (col == lanes)
    present_row = jnp.max(present.astype(F32), axis=0, keepdims=True)
    ci = iota((coarse_n, coarse_n), 0)
    cj = iota((coarse_n, coarse_n), 1)
    local_col = jnp.sum(jnp.where(cj < ci, present_row, 0.0), axis=1, keepdims=True)
    present_col = jnp.sum(jnp.where(cj == ci, present_row, 0.0), axis=1, keepdims=True)
    slot_i = iota((coarse_n, group_slots), 1)
    slot_local = (slot_i % slot_w // MOST).astype(F32)
    e_hit = (local_col == slot_local) & (present_col > 0.5)
    e_mat = e_hit.astype(BF)
    slot_cluster = jnp.sum(
        jnp.where(e_hit, iota((coarse_n, group_slots), 0), 0), axis=0, keepdims=True
    )
    slot_cluster = jnp.concatenate([slot_cluster] * groups, axis=1)

    ids_t = jnp.transpose(ids_ref[...].astype(F32))
    kk = ids_ref.shape[0] // senders
    row_lane = iota((per_sender, coarse_n), 1).astype(F32)
    for s in range(senders):
        hit = jnp.zeros((per_sender, coarse_n), jnp.bool_)
        for k in range(MOST):
            hit = hit | (ids_t[:per_sender, s * kk + k : s * kk + k + 1] == row_lane)
        match[pl.ds(s * per_sender, per_sender), :] = hit.astype(F32)
    step = 256
    ri = iota((step, step), 0)
    rj = iota((step, step), 1)
    lower = ((rj <= ri) & (rj // per_sender == ri // per_sender)).astype(BF)
    for b in range(total // step):
        m = match[pl.ds(b * step, step), :]
        upto = jnp.dot(lower, m.astype(BF), preferred_element_type=F32)
        mrank[pl.ds(b * step, step), :] = (upto * m).astype(BF)
    want = (iota((group_rows, group_slots), 1) % MOST + 1).astype(F32)
    same = (
        iota((group_rows, group_slots), 0) // per_sender
        == iota((group_rows, group_slots), 1) // slot_w
    )
    for b in range(groups):
        part = pl.ds(b * group_rows, group_rows)
        rank_e = jnp.dot(mrank[part, :], e_mat, preferred_element_type=F32)
        pick = (rank_e == want) & same
        sel[part, :] = pick.astype(BF)
        arrived[pl.ds(b * group_slots, group_slots), :] = lax.dot_general(
            pick.astype(BF), rows_ref[part, :], TN, preferred_element_type=F32
        ).astype(BF)

    ones = jnp.ones((total, 128), BF)
    for turn in range(ITERS):
        c_ref = coarse_ref if turn == 0 else coarse_out
        f_ref = fine_ref if turn == 0 else cent
        to_ref = fine_out if turn == ITERS - 1 else cent
        cf = c_ref[...].astype(F32)
        half = 0.5 * jnp.sum(cf * cf, axis=1, keepdims=True)
        half_row = jnp.sum(jnp.where(ci == cj, half, 0.0), axis=0, keepdims=True)
        dots = lax.dot_general(rows_ref[...], c_ref[...], NT, preferred_element_type=F32)
        masked = jnp.where(match[...] > 0.5, (dots - half_row) * scale, -jnp.inf)
        top = jnp.max(masked, axis=1, keepdims=True)
        ex = jnp.exp(masked - top)
        qb = (ex / jnp.sum(ex, axis=1, keepdims=True)).astype(BF)
        qbuf[...] = qb
        csum = lax.dot_general(qb, rows_ref[...], TN, preferred_element_type=F32)
        cmass = lax.dot_general(qb, ones, TN, preferred_element_type=F32)[:, :1]
        coarse_out[...] = ((csum + prior * cf) / (cmass + prior)).astype(BF)

        slot_q = []
        for b in range(groups):
            part = pl.ds(b * group_rows, group_rows)
            qe = jnp.dot(qbuf[part, :], e_mat, preferred_element_type=F32)
            slot_q.append(
                jnp.sum(qe * sel[part, :].astype(F32), axis=0, keepdims=True)
            )
        slot_q = jnp.concatenate(slot_q, axis=1)

        best = jnp.full((1, slots), -jnp.inf, F32)
        for b in range(tiles):
            part = pl.ds(b * tile, tile)
            ft = f_ref[part, :]
            ff = ft.astype(F32)
            norm = 0.5 * jnp.sum(ff * ff, axis=1, keepdims=True)
            d = lax.dot_general(ft, arrived[...], NT, preferred_element_type=F32)
            allowed = parent_col[part, :1] == slot_cluster
            l = jnp.where(allowed, (d - norm) * (scale * log2e), -jnp.inf)
            logit[part, :] = l
            best = jnp.maximum(best, jnp.max(l, axis=0, keepdims=True))
        denom = jnp.zeros((1, slots), F32)
        for b in range(tiles):
            part = pl.ds(b * tile, tile)
            e = jnp.exp2(logit[part, :] - best)
            logit[part, :] = e
            denom = denom + jnp.sum(e, axis=0, keepdims=True)
        factor = slot_q / denom
        for b in range(tiles):
            part = pl.ds(b * tile, tile)
            resp = logit[part, :] * factor
            mass = jnp.sum(resp, axis=1, keepdims=True)
            fsum = jnp.dot(resp.astype(BF), arrived[...], preferred_element_type=F32)
            to_ref[part, :] = (
                (fsum + f_ref[part, :].astype(F32)) * (1.0 / (mass + 1.0))
            ).astype(BF)


def update(senders, per_sender, rows, ids, parent, fine, coarse):
    total, width = rows.shape
    coarse_n = coarse.shape[0]
    block = fine.shape[0]
    owned = coarse_n // senders
    slots = senders * owned * MOST
    group_slots = max(1, 128 // (owned * MOST)) * owned * MOST
    return pl.pallas_call(
        functools.partial(update_kernel, senders, per_sender, owned),
        out_shape=(
            jax.ShapeDtypeStruct(fine.shape, BF),
            jax.ShapeDtypeStruct(coarse.shape, BF),
        ),
        in_specs=[pl.BlockSpec(memory_space=pltpu.VMEM)] * 5,
        out_specs=(pl.BlockSpec(memory_space=pltpu.VMEM),) * 2,
        scratch_shapes=[
            pltpu.VMEM((total, coarse_n), F32),
            pltpu.VMEM((total, coarse_n), BF),
            pltpu.VMEM((total, coarse_n), BF),
            pltpu.VMEM((slots, width), BF),
            pltpu.VMEM((block, slots), F32),
            pltpu.VMEM((block, width), BF),
            pltpu.VMEM((block, 128), jnp.int32),
            pltpu.VMEM((total, group_slots), BF),
        ],
        compiler_params=pltpu.CompilerParams(vmem_limit_bytes=56 * 2**20),
    )(rows, ids, parent, fine, coarse)


def on_device(rows, coarse_ids, parent, fine_cent, coarse_cent):
    nz = lax.axis_size("dp")
    nc = lax.axis_size("cent")
    senders = nz * nc
    per_sender, width = rows.shape
    ids = jnp.pad(
        coarse_ids.T, ((0, 8 - coarse_ids.shape[1]), (0, 128 - per_sender)), constant_values=-1
    )
    rows_all, ids_all = gather(nz, nc, rows, ids)
    return update(
        senders,
        per_sender,
        rows_all.reshape(senders * per_sender, width),
        ids_all.reshape(senders * 8, 128),
        parent.reshape(-1, 128),
        fine_cent,
        coarse_cent,
    )


def solution(mesh):
    in_specs = (
        P(("groups", "dp", "cent"), None),
        P(("groups", "dp", "cent"), None),
        P("groups"),
        P(("groups", "dp", "cent"), None),
        P("groups", None),
    )
    out_specs = (P(("groups", "dp", "cent"), None), P("groups", None))
    return jax.shard_map(
        on_device, mesh=mesh, in_specs=in_specs, out_specs=out_specs, check_vma=False
    )
```

time: 141 us -> 52.8 us (0.37)
  Pallas kernels: 0 us -> 48.5 us
  blocking collectives: 45.8 us -> 0 us
  matrix products: 23.8 us -> 0 us
  other arithmetic: 18.3 us -> 0 us
  local copies, waits for them, and re-layouts: 20 us -> 3.53 us
  waiting for transfers between devices: 16.4 us -> 0 us
  starting transfers between devices: 14.7 us -> 0 us
    pallas_call x0 -> x2, Pallas kernels: none -> 48.5 us  [the longest x1 24.7 us: update(): pl.pallas_call(functools.partial(update_kernel, senders, per_sender, owne...]
    all_gather x2 -> x0, blocking collectives: 45.8 us -> none  [on_device(): collected = lax.all_gather(updated, ('dp', 'cent'), axis=0, tiled=True)]
    dot_general x16 -> x0, matrix products: 23.8 us -> none  [the longest x2 9.97 us: owner_update(): lax.dot_general(resp_b, arrived, (((0,), (0,)), ((), ())), preferred_elem...]
    all_to_all x3 -> x0, waiting for transfers between devices: 16.4 us -> none  [the longest x1 11.9 us: send_both(): lax.all_to_all(outgoing, ('dp', 'cent'), split_axis=0, concat_axis=0, til...]
    all_to_all x3 -> x0, starting transfers between devices: 14.7 us -> none  [the longest x1 7.36 us: send_both(): lax.all_to_all(outgoing_q, ('dp', 'cent'), split_axis=0, concat_axis=0, t...]
    unnamed x17 -> x6, local copies, waits for them, and re-layouts: 15.9 us -> 2.84 us
    reduce_sum x18 -> x0, other arithmetic: 12.2 us -> none  [the longest x2 4.27 us: owner_update(): mass = jnp.sum(resp, axis=0)]
    reduce_or x2 -> x0, other arithmetic: 5.84 us -> none  [the longest x1 5.69 us: route_tables(): present = jnp.any(blocks[:, :, None] == cluster_ids[None, None, :], axis=1)]
  transfers between devices with their start and end apart: 3 -> 0, of which waited for: 2 -> 0; matrix products, arithmetic and copies ran while one was open for 19% -> 0% of each run, Pallas kernels for 0% -> 0%
where the time goes in v1:
time: 52.8 us; the launch traced here: 52.7 us
  Pallas kernels  48.5 us (92%)
  local copies, waits for them, and re-layouts  3.53 us (7%)
  between operations  0.65 us (1%)
    pallas_call x1, Pallas kernels, update(): pl.pallas_call(functools.partial(update_kernel, senders, per_sender, owne...  24.7 us
    pallas_call x1, Pallas kernels, gather(): pl.pallas_call(functools.partial(gather_kernel, nz, nc), out_shape=(jax.S...  23.8 us
    unnamed x6, local copies, waits for them, and re-layouts  2.84 us

profile of v1, /device:TPU:0, one launch (start us, length us, event | category | flops | bytes accessed | tf_op | source)
XLA Modules:
  0.0 52.7 jit_solution(740397813196756754)
XLA Ops:
  0.6 0.7 %pad.4.ids_ref = s32[8,128]{1,0:T(8,128)S(1)} pad(s32[4,64]{1,0:T(4,128)} %bitcast.7, s32[]{:T(128)} %constant.0.clone.1), padding=0_4x0_64 | pad | bytes 5124 | tf_op jit(solution)/shard_map/jit(_pad)/pad | solution.py:335
  1.3 0.0 copy-start.1
  1.3 0.9 %copy-done.1 = bf16[64,1024]{1,0:T(8,128)(2,1)S(1)} copy-done((bf16[64,1024]{1,0:T(8,128)(2,1)S(1)}, bf16[64,1024]{1,0:T(8,128)(2,1)}, u32[]{:S(2)}) %copy-start.1) | copy-done | bytes 131096
  2.2 23.8 %shard_map.68 = (bf16[4,4,64,1024]{3,2,1,0:T(8,128)(2,1)S(1)}, s32[4,4,8,128]{3,2,1,0:T(8,128)S(1)}) custom-call(bf16[64,1024]{1,0:T(8,128)(2,1)S(1)} %copy-done.1, s32[8,128]{1,0:T(8,128)S(1)} %pad.4.ids_ref), custom_call_target="tpu_custom_call" | custom-call | tf_op jit(solution)/shard_map/pallas_call | solution.py:146
  26.0 0.0 copy-start
  26.0 1.3 %copy-done = bf16[4,4,64,1024]{3,2,1,0:T(8,128)(2,1)} copy-done((bf16[4,4,64,1024]{3,2,1,0:T(8,128)(2,1)}, bf16[4,4,64,1024]{3,2,1,0:T(8,128)(2,1)S(1)}, u32[]{:S(2)}) %copy-start) | copy-done | bytes 2097176
  27.4 0.0 copy-start.2
  27.4 0.6 %copy-done.2 = s32[4,4,8,128]{3,2,1,0:T(8,128)} copy-done((s32[4,4,8,128]{3,2,1,0:T(8,128)}, s32[4,4,8,128]{3,2,1,0:T(8,128)S(1)}, u32[]{:S(2)}) %copy-start.2) | copy-done | bytes 65560
  28.0 24.7 %shard_map.69 = (bf16[2048,1024]{1,0:T(8,128)(2,1)}, bf16[128,1024]{1,0:T(8,128)(2,1)}) custom-call(bf16[1024,1024]{1,0:T(8,128)(2,1)} %bitcast.4, s32[128,128]{1,0:T(8,128)} %bitcast.5, s32[256,128]{1,0:T(8,128)} %bitcast.6, bf16[2048,1024]{1,0:T(8,128)(2,1)} %fine_ref.1, bf16[128,1024]{1,0:T(8,128)(2,1)} %coarse_ref.1), custom_call_target="tpu_custom_call" | custom-call | tf_op jit(solution)/shard_map/pallas_call | solution.py:308
Async XLA Ops:
  1.3 0.9 %copy-start.1 = (bf16[64,1024]{1,0:T(8,128)(2,1)S(1)}, bf16[64,1024]{1,0:T(8,128)(2,1)}, u32[]{:S(2)}) copy-start(bf16[64,1024]{1,0:T(8,128)(2,1)} %rows_ref.1) | copy-start | bytes 393220
  26.0 1.3 %copy-start = (bf16[4,4,64,1024]{3,2,1,0:T(8,128)(2,1)}, bf16[4,4,64,1024]{3,2,1,0:T(8,128)(2,1)S(1)}, u32[]{:S(2)}) copy-start(bf16[4,4,64,1024]{3,2,1,0:T(8,128)(2,1)S(1)} %get-tuple-element.4) | copy-start | bytes 6291460
  27.4 0.6 %copy-start.2 = (s32[4,4,8,128]{3,2,1,0:T(8,128)}, s32[4,4,8,128]{3,2,1,0:T(8,128)S(1)}, u32[]{:S(2)}) copy-start(s32[4,4,8,128]{3,2,1,0:T(8,128)S(1)} %get-tuple-element.5) | copy-start | bytes 196612

commit v2 on v1

v2 whole, which is shorter than its diff:
```python
import functools
import math

import jax
import jax.numpy as jnp
from jax import lax
from jax.experimental import pallas as pl
from jax.experimental.pallas import tpu as pltpu
from jax.sharding import PartitionSpec as P

ITERS = 2
MOST = 4
VMEM_LIMIT = 60 * 2**20
BF = jnp.bfloat16
F32 = jnp.float32
NT = (((1,), (1,)), ((), ()))
TN = (((0,), (0,)), ((), ()))


def iota(shape, dim):
    return lax.broadcasted_iota(jnp.int32, shape, dim)


def first_kernel(
    nz, nc, owned, rows_ref, ids_hbm, parent_hbm, fine_hbm, coarse_hbm,
    f1_out, arrived_out, pcol_out, scl_hbm, sq_hbm, c2_hbm,
    arrived, pcol, scl_out, sq_out, c2_out,
    rows_all, ids_all, match, sel, norms, logit, facc, masses, csum, cmass, c1, sq_first,
    ids_ref, parent_ref, fine_ref, coarse_ref,
    rsend, rrecv, isend, irecv, local_sem, out_sem,
):
    per_sender, width = rows_ref.shape
    senders = nz * nc
    total = senders * per_sender
    coarse_n = coarse_ref.shape[0]
    block = fine_ref.shape[0]
    tops = ids_hbm.shape[0]
    slot_w = owned * MOST
    scale = 1.0 / math.sqrt(width)
    scale2 = scale * math.log2(math.e)
    prior = float(max(1, total // coarse_n))
    per_group = 128 // slot_w
    planes = per_group // nc
    group_rows = per_group * per_sender
    groups = senders // per_group
    tile = min(512, block)
    tiles = block // tile
    parts = [pl.ds(b * tile, tile) for b in range(tiles)]
    interleave = planes == 1

    nx = nc // 2
    g = lax.axis_index("groups")
    z = lax.axis_index("dp")
    ce = lax.axis_index("cent")
    x = ce // 2
    core = ce % 2
    other = x * 2 + (1 - core)
    here = lambda zz, cc: (g, zz, cc)

    barrier = pltpu.get_barrier_semaphore()
    links = [
        (z > 0, here(z - 1, ce)),
        (z < nz - 1, here(z + 1, ce)),
        (x > 0, here(z, ce - 2)),
        (x < nx - 1, here(z, ce + 2)),
    ]
    for ok, dev in links:
        @pl.when(ok)
        def _():
            pl.semaphore_signal(barrier, inc=1, device_id=dev, device_id_type=pl.DeviceIdType.MESH)
    pl.semaphore_signal(
        barrier, inc=1, device_id=here(z, other), device_id_type=pl.DeviceIdType.MESH
    )
    loads = [
        pltpu.make_async_copy(a, b, local_sem.at[i])
        for i, (a, b) in enumerate(
            [
                (rows_ref, rows_all.at[z, ce]),
                (ids_hbm, ids_ref),
                (coarse_hbm, coarse_ref),
                (parent_hbm, parent_ref),
                (fine_hbm, fine_ref),
            ]
        )
    ]
    for load in loads:
        load.start()
    degree = 1 + sum(ok.astype(jnp.int32) for ok, _ in links)
    loads[1].wait()
    ids_all[z, ce] = jnp.full((8, 128), -1, jnp.int32)
    ids_all[z, ce, :tops, :per_sender] = ids_ref[...]
    loads[0].wait()
    pl.semaphore_wait(barrier, degree)

    def copies(zc, cc, way, dev):
        out = []
        for buf, ss, rs in ((rows_all, rsend, rrecv), (ids_all, isend, irecv)):
            out.append(
                pltpu.make_async_remote_copy(
                    src_ref=buf.at[zc, cc],
                    dst_ref=buf.at[zc, cc],
                    send_sem=ss.at[way, zc, cc],
                    recv_sem=rs.at[zc, cc],
                    device_id=dev,
                    device_id_type=pl.DeviceIdType.MESH,
                )
            )
        return out

    def send(zc, cc, way, dev, ok=None):
        def go():
            for c in copies(zc, cc, way, dev):
                c.start()
        if ok is None:
            go()
        else:
            pl.when(ok)(go)

    def wait_in(zc, cc):
        for c in copies(zc, cc, 0, here(z, other)):
            c.wait_recv()

    def on_x(zc, xc, right, left):
        cc = xc * 2 + core
        send(zc, cc, 3, here(z, ce + 2), right & (x < nx - 1))
        send(zc, cc, 2, here(z, ce - 2), left & (x > 0))
        send(zc, cc, 4, here(z, other))

    true = z >= 0

    def z_chunk(zc, up, down):
        send(zc, ce, 1, here(z + 1, ce), up & (z < nz - 1))
        send(zc, ce, 0, here(z - 1, ce), down & (z > 0))
        on_x(zc, x, true, true)

    def each_z(d, fn):
        if d == 0:
            fn(z, 0)
            return
        for sign in (-1, 1):
            zc = z + sign * d
            @pl.when((zc >= 0) & (zc < nz))
            def _():
                fn(zc, sign)

    def z_step(zc, sign):
        if sign == 0:
            z_chunk(zc, true, true)
        else:
            wait_in(zc, ce)
            z_chunk(zc, true if sign < 0 else ~true, true if sign > 0 else ~true)

    def comm_step(t):
        if t < nz:
            each_z(t, z_step)
        for e in range(1, nx):
            d = t - e
            if d < 0 or d >= nz:
                continue
            for sign in (-1, 1):
                xc = x + sign * e
                @pl.when((xc >= 0) & (xc < nx))
                def _():
                    def one(zc, _):
                        wait_in(zc, xc * 2 + core)
                        on_x(zc, xc, true if sign < 0 else ~true, true if sign > 0 else ~true)
                    each_z(d, one)

    def wait_other(zc):
        for xc in range(nx):
            wait_in(zc, xc * 2 + (1 - core))

    comm_step(0)

    loads[3].wait()
    own_rows = block // 128
    me = z * nc + ce
    own = parent_ref[pl.ds(pl.multiple_of(me * own_rows, own_rows), own_rows), :]
    if own_rows < 8:
        own = jnp.concatenate([own] * (8 // own_rows), axis=0)
    own_t = jnp.transpose(own.astype(F32))
    present = jnp.zeros((128, coarse_n), jnp.bool_)
    lanes = iota((128, coarse_n), 1)
    for b in range(own_rows):
        col = own_t[:, b : b + 1].astype(jnp.int32)
        pcol[pl.ds(b * 128, 128), :] = jnp.broadcast_to(col, (128, 128))
        present = present | (col == lanes)
    present_row = jnp.max(present.astype(F32), axis=0, keepdims=True)
    ci = iota((coarse_n, coarse_n), 0)
    cj = iota((coarse_n, coarse_n), 1)
    local_col = jnp.sum(jnp.where(cj < ci, present_row, 0.0), axis=1, keepdims=True)
    present_col = jnp.sum(jnp.where(cj == ci, present_row, 0.0), axis=1, keepdims=True)
    slot_local = (iota((coarse_n, 128), 1) % slot_w // MOST).astype(F32)
    e_hit = (local_col == slot_local) & (present_col > 0.5)
    e_mat = e_hit.astype(BF)
    slot_cluster = jnp.sum(jnp.where(e_hit, iota((coarse_n, 128), 0), 0), axis=0, keepdims=True)
    scl_out[...] = jnp.broadcast_to(slot_cluster, (8, 128))
    outs = [pltpu.make_async_copy(pcol, pcol_out, out_sem.at[0])]
    outs[0].start()
    outs.append(pltpu.make_async_copy(scl_out, scl_hbm, out_sem.at[1]))
    outs[1].start()
    step = 256
    ri = iota((step, step), 0)
    rj = iota((step, step), 1)
    lower = ((rj <= ri) & (rj // per_sender == ri // per_sender)).astype(BF)
    want = (iota((group_rows, 128), 1) % MOST + 1).astype(F32)
    same = iota((group_rows, 128), 0) // per_sender == iota((group_rows, 128), 1) // slot_w
    row_lane = iota((per_sender, coarse_n), 1).astype(F32)
    ones = jnp.ones((group_rows, 128), BF)

    def half_row_of(c_ref):
        cf = c_ref[...].astype(F32)
        half = 0.5 * jnp.sum(cf * cf, axis=1, keepdims=True)
        return jnp.sum(jnp.where(ci == cj, half, 0.0), axis=0, keepdims=True)

    def rows_of(b):
        return rows_all[pl.ds(b * planes, planes)].reshape(group_rows, width)

    def span(b, size):
        return pl.ds(pl.multiple_of(b * size, size), size)

    def coarse_group(b, rows_g, c_ref, half_row, hit):
        dots = lax.dot_general(rows_g, c_ref[...], NT, preferred_element_type=F32)
        masked = jnp.where(hit > 0.5, (dots - half_row) * scale, -jnp.inf)
        top = jnp.max(masked, axis=1, keepdims=True)
        ex = jnp.exp(masked - top)
        qb = (ex / jnp.sum(ex, axis=1, keepdims=True)).astype(BF)
        csum[...] += lax.dot_general(qb, rows_g, TN, preferred_element_type=F32)
        cmass[...] += lax.dot_general(qb, ones, TN, preferred_element_type=F32)
        qe = jnp.dot(qb, e_mat, preferred_element_type=F32)
        return jnp.sum(
            qe * sel[span(b, group_rows), :].astype(F32), axis=0, keepdims=True
        )

    def coarse_end(c_ref, to_ref):
        to_ref[...] = (
            (csum[...] + prior * c_ref[...].astype(F32)) / (cmass[:, :1] + prior)
        ).astype(BF)

    loads[2].wait()
    half_first = half_row_of(coarse_ref)
    csum[...] = jnp.zeros_like(csum)
    cmass[...] = jnp.zeros_like(cmass)

    def prep(b):
        rows_g = rows_of(b)
        ids_t = jnp.transpose(
            ids_all[pl.ds(b * planes, planes)].reshape(per_group * 8, 128).astype(F32)
        )
        hits = []
        for s in range(per_group):
            hit = jnp.zeros((per_sender, coarse_n), jnp.bool_)
            for k in range(MOST):
                hit = hit | (ids_t[:per_sender, s * 8 + k : s * 8 + k + 1] == row_lane)
            hits.append(hit.astype(F32))
        hit = jnp.concatenate(hits, axis=0)
        match[span(b, group_rows), :] = hit
        ranks = []
        for i in range(group_rows // step):
            m = hit[i * step : (i + 1) * step]
            upto = jnp.dot(lower, m.astype(BF), preferred_element_type=F32)
            ranks.append((upto * m).astype(BF))
        rank = jnp.concatenate(ranks, axis=0)
        rank_e = jnp.dot(rank, e_mat, preferred_element_type=F32)
        pick = ((rank_e == want) & same).astype(BF)
        sel[span(b, group_rows), :] = pick
        slots_g = lax.dot_general(pick, rows_g, TN, preferred_element_type=F32).astype(BF)
        arrived[span(b, 128), :] = slots_g
        slot_q = coarse_group(b, rows_g, coarse_ref, half_first, hit)
        sq_first[b] = jnp.broadcast_to(slot_q, (8, 128))

    cluster2 = jnp.concatenate([slot_cluster] * 2, axis=1)
    twice = lambda v: jnp.concatenate([v, v], axis=1)

    def pair_slots(b0, b1):
        return jnp.concatenate([arrived[span(b0, 128), :], arrived[span(b1, 128), :]], axis=0)

    def pair_prob(b0, b1):
        slots_g = pair_slots(b0, b1)
        best = jnp.full((1, 256), -jnp.inf, F32)
        for part in parts:
            d = lax.dot_general(fine_ref[part, :], slots_g, NT, preferred_element_type=F32)
            l = jnp.where(
                twice(pcol[part, :]) == cluster2, (d - twice(norms[part, :])) * scale2, -jnp.inf
            )
            logit[part, :] = l
            best = jnp.maximum(best, jnp.max(l, axis=0, keepdims=True))
        denom = jnp.zeros((1, 256), F32)
        for part in parts:
            e = jnp.exp2(logit[part, :] - best)
            logit[part, :] = e
            denom = denom + jnp.sum(e, axis=0, keepdims=True)
        return jnp.concatenate([sq_first[b0][:1], sq_first[b1][:1]], axis=1) / denom

    def pair_sum(i, b0, b1, factor):
        slots_g = pair_slots(b0, b1)
        for part in parts:
            resp = logit[part, :] * factor
            fsum = jnp.dot(resp.astype(BF), slots_g, preferred_element_type=F32)
            mass = resp[:, :128] + resp[:, 128:]
            if i > 0:
                fsum = fsum + facc[part, :]
                mass = mass + masses[part, :]
            if i < groups // 2 - 1:
                facc[part, :] = fsum
                masses[part, :] = mass
            else:
                fine_ref[part, :] = (
                    (fsum + fine_ref[part, :].astype(F32))
                    * (1.0 / (jnp.sum(mass, axis=1, keepdims=True) + 1.0))
                ).astype(BF)
                outs.append(
                    pltpu.make_async_copy(
                        fine_ref.at[part, :], f1_out.at[part, :], out_sem.at[len(outs)]
                    )
                )
                outs[-1].start()

    def arrived_copy():
        outs.append(pltpu.make_async_copy(arrived, arrived_out, out_sem.at[len(outs)]))
        outs[-1].start()

    def fill_norms():
        loads[4].wait()
        for part in parts:
            ff = fine_ref[part, :].astype(F32)
            half = 0.5 * jnp.sum(ff * ff, axis=1, keepdims=True)
            norms[part, :] = jnp.broadcast_to(half, (tile, 128))

    last = nz + nx - 1
    if interleave:
        up = z < nz // 2
        order = [jnp.where(up, (z + k) % nz, (z - k + nz) % nz) for k in range(nz)]
        pairs = [(order[2 * i], order[2 * i + 1]) for i in range(nz // 2)]
        for t in range(1, last):
            comm_step(t)
            k = t - (nx - 1)
            if k == 0:
                fill_norms()
            if 0 <= k < nz // 2:
                wait_other(order[k])
                prep(order[k])
            elif k == nz // 2:
                pair_sum(0, *pairs[0], pair_prob(*pairs[0]))
        for k in range(nz // 2, nz):
            wait_other(order[k])
            prep(order[k])
        arrived_copy()
        for i in range(1, nz // 2):
            pair_sum(i, *pairs[i], pair_prob(*pairs[i]))
    else:
        fill_norms()
        for t in range(1, last):
            comm_step(t)
        for t in range(nz):
            each_z(t, lambda zc, _: wait_other(zc))
        lax.fori_loop(0, groups, lambda b, c: (prep(b), c)[1], 0)
        arrived_copy()
        for i in range(groups // 2):
            pair_sum(i, 2 * i, 2 * i + 1, pair_prob(2 * i, 2 * i + 1))

    coarse_end(coarse_ref, c1)
    half_second = half_row_of(c1)
    csum[...] = jnp.zeros_like(csum)
    cmass[...] = jnp.zeros_like(cmass)

    def second(b):
        slot_q = coarse_group(b, rows_of(b), c1, half_second, match[span(b, group_rows), :])
        sq_out[b] = jnp.broadcast_to(slot_q, (8, 128))

    if interleave:
        rows_g = rows_all[...].reshape(total, width)
        dots = lax.dot_general(rows_g, c1[...], NT, preferred_element_type=F32)
        masked = jnp.where(match[...] > 0.5, (dots - half_second) * scale, -jnp.inf)
        ex = jnp.exp(masked - jnp.max(masked, axis=1, keepdims=True))
        qb = (ex * (1.0 / jnp.sum(ex, axis=1, keepdims=True))).astype(BF)
        csum[...] = lax.dot_general(qb, rows_g, TN, preferred_element_type=F32)
        mass_row = jnp.sum(qb.astype(F32), axis=0, keepdims=True)
        mass_col = jnp.sum(jnp.where(ci == cj, mass_row, 0.0), axis=1, keepdims=True)
        cmass[...] = jnp.broadcast_to(mass_col, cmass.shape)
        qe = jnp.dot(qb, e_mat, preferred_element_type=F32) * sel[...].astype(F32)
        for b in range(groups):
            slot_q = jnp.sum(
                qe[b * group_rows : (b + 1) * group_rows], axis=0, keepdims=True
            )
            sq_out[b] = jnp.broadcast_to(slot_q, (8, 128))
    else:
        lax.fori_loop(0, groups, lambda b, c: (second(b), c)[1], 0)
    coarse_end(c1, c2_out)

    for src, dst in ((sq_out, sq_hbm), (c2_out, c2_hbm)):
        outs.append(pltpu.make_async_copy(src, dst, out_sem.at[len(outs)]))
        outs[-1].start()
    for c in outs:
        c.wait()
    def sent(zc, cc, way, ok):
        @pl.when(ok)
        def _():
            for c in copies(zc, cc, way, here(z, other)):
                c.wait_send()
    for zc in range(nz):
        sent(zc, ce, 1, (zc <= z) & (z < nz - 1))
        sent(zc, ce, 0, (zc >= z) & (z > 0))
        for xc in range(nx):
            cc = xc * 2 + core
            sent(zc, cc, 3, (xc <= x) & (x < nx - 1))
            sent(zc, cc, 2, (xc >= x) & (x > 0))
            sent(zc, cc, 4, true)


def first(nz, nc, rows, ids, parent, fine, coarse):
    per_sender, width = rows.shape
    senders = nz * nc
    total = senders * per_sender
    coarse_n = coarse.shape[0]
    block = fine.shape[0]
    owned = coarse_n // senders
    slots = senders * owned * MOST
    groups = slots // 128
    return pl.pallas_call(
        functools.partial(first_kernel, nz, nc, owned),
        out_shape=(
            jax.ShapeDtypeStruct(fine.shape, BF),
            jax.ShapeDtypeStruct((slots, width), BF),
            jax.ShapeDtypeStruct((block, 128), jnp.int32),
            jax.ShapeDtypeStruct((8, 128), jnp.int32),
            jax.ShapeDtypeStruct((groups, 8, 128), F32),
            jax.ShapeDtypeStruct(coarse.shape, BF),
        ),
        in_specs=[pl.BlockSpec(memory_space=pltpu.HBM)] * 5,
        out_specs=(pl.BlockSpec(memory_space=pltpu.HBM),) * 6,
        scratch_shapes=[
            pltpu.VMEM((slots, width), BF),
            pltpu.VMEM((block, 128), jnp.int32),
            pltpu.VMEM((8, 128), jnp.int32),
            pltpu.VMEM((groups, 8, 128), F32),
            pltpu.VMEM(coarse.shape, BF),
            pltpu.VMEM((nz, nc) + rows.shape, BF),
            pltpu.VMEM((nz, nc, 8, 128), jnp.int32),
            pltpu.VMEM((total, coarse_n), F32),
            pltpu.VMEM((total, 128), BF),
            pltpu.VMEM((block, 128), F32),
            pltpu.VMEM((block, 256), F32),
            pltpu.VMEM(fine.shape, F32),
            pltpu.VMEM((block, 128), F32),
            pltpu.VMEM(coarse.shape, F32),
            pltpu.VMEM((coarse_n, 128), F32),
            pltpu.VMEM(coarse.shape, BF),
            pltpu.VMEM((groups, 8, 128), F32),
            pltpu.VMEM(ids.shape, jnp.int32),
            pltpu.VMEM(parent.shape, jnp.int32),
            pltpu.VMEM(fine.shape, BF),
            pltpu.VMEM(coarse.shape, BF),
            pltpu.SemaphoreType.DMA((5, nz, nc)),
            pltpu.SemaphoreType.DMA((nz, nc)),
            pltpu.SemaphoreType.DMA((5, nz, nc)),
            pltpu.SemaphoreType.DMA((nz, nc)),
            pltpu.SemaphoreType.DMA((5,)),
            pltpu.SemaphoreType.DMA((5 + max(1, block // 512),)),
        ],
        compiler_params=pltpu.CompilerParams(
            collective_id=0,
            has_side_effects=True,
            vmem_limit_bytes=VMEM_LIMIT,
        ),
    )(rows, ids, parent, fine, coarse)


def second_kernel(
    f1_hbm, arrived_hbm, pcol_hbm, scl_hbm, sq_hbm, c2_hbm, fine_out, coarse_out,
    scl_ref, sq_ref, logit, result, f1_ref, arrived, pcol, sems, in_sems,
):
    block, width = f1_hbm.shape
    groups = sq_hbm.shape[0]
    slots = groups * 128
    scale2 = math.log2(math.e) / math.sqrt(width)
    tile = min(512, block)
    parts = [pl.ds(b * tile, tile) for b in range(block // tile)]
    small = [
        pltpu.make_async_copy(a, b, in_sems.at[i])
        for i, (a, b) in enumerate(
            [(arrived_hbm, arrived), (scl_hbm, scl_ref), (sq_hbm, sq_ref), (c2_hbm, coarse_out)]
        )
    ]
    for c in small:
        c.start()
    loads = []
    for b, part in enumerate(parts):
        loads.append(
            [
                pltpu.make_async_copy(src.at[part, :], dst.at[part, :], in_sems.at[4 + 2 * b + i])
                for i, (src, dst) in enumerate([(f1_hbm, f1_ref), (pcol_hbm, pcol)])
            ]
        )
        for c in loads[-1]:
            c.start()
    for c in small[:3]:
        c.wait()
    slot_cluster = jnp.concatenate([scl_ref[:1, :]] * groups, axis=1)
    slot_q = jnp.concatenate([sq_ref[b, :1, :] for b in range(groups)], axis=1)
    best = jnp.full((1, slots), -jnp.inf, F32)
    for part, pending in zip(parts, loads):
        for c in pending:
            c.wait()
        ft = f1_ref[part, :]
        ff = ft.astype(F32)
        norm = 0.5 * jnp.sum(ff * ff, axis=1, keepdims=True)
        d = lax.dot_general(ft, arrived[...], NT, preferred_element_type=F32)
        same = jnp.concatenate([pcol[part, :]] * groups, axis=1) == slot_cluster
        l = jnp.where(same, (d - norm) * scale2, -jnp.inf)
        logit[part, :] = l
        best = jnp.maximum(best, jnp.max(l, axis=0, keepdims=True))
    denom = jnp.zeros((1, slots), F32)
    for part in parts:
        e = jnp.exp2(logit[part, :] - best)
        logit[part, :] = e
        denom = denom + jnp.sum(e, axis=0, keepdims=True)
    factor = slot_q / denom
    copies = [small[3]]
    for b, part in enumerate(parts):
        resp = logit[part, :] * factor
        mass = jnp.sum(resp, axis=1, keepdims=True)
        fsum = jnp.dot(resp.astype(BF), arrived[...], preferred_element_type=F32)
        result[part, :] = (
            (fsum + f1_ref[part, :].astype(F32)) * (1.0 / (mass + 1.0))
        ).astype(BF)
        copies.append(pltpu.make_async_copy(result.at[part, :], fine_out.at[part, :], sems.at[b]))
        copies[-1].start()
    for c in copies:
        c.wait()


def second(f1, arrived, pcol, scl, sq, c2):
    block, width = f1.shape
    slots = arrived.shape[0]
    return pl.pallas_call(
        second_kernel,
        out_shape=(jax.ShapeDtypeStruct(f1.shape, BF), jax.ShapeDtypeStruct(c2.shape, BF)),
        in_specs=[pl.BlockSpec(memory_space=pltpu.HBM)] * 6,
        out_specs=(pl.BlockSpec(memory_space=pltpu.HBM),) * 2,
        scratch_shapes=[
            pltpu.VMEM(scl.shape, jnp.int32),
            pltpu.VMEM(sq.shape, F32),
            pltpu.VMEM((block, slots), F32),
            pltpu.VMEM((block, width), BF),
            pltpu.VMEM((block, width), BF),
            pltpu.VMEM((slots, width), BF),
            pltpu.VMEM((block, 128), jnp.int32),
            pltpu.SemaphoreType.DMA((max(1, block // 512),)),
            pltpu.SemaphoreType.DMA((4 + 2 * max(1, block // 512),)),
        ],
        compiler_params=pltpu.CompilerParams(vmem_limit_bytes=VMEM_LIMIT),
    )(f1, arrived, pcol, scl, sq, c2)


def on_device(rows, coarse_ids, parent, fine_cent, coarse_cent):
    nz = lax.axis_size("dp")
    nc = lax.axis_size("cent")
    return second(*first(nz, nc, rows, coarse_ids.T, parent.reshape(-1, 128), fine_cent, coarse_cent))


def solution(mesh):
    in_specs = (
        P(("groups", "dp", "cent"), None),
        P(("groups", "dp", "cent"), None),
        P("groups"),
        P(("groups", "dp", "cent"), None),
        P("groups", None),
    )
    out_specs = (P(("groups", "dp", "cent"), None), P("groups", None))
    return jax.shard_map(
        on_device, mesh=mesh, in_specs=in_specs, out_specs=out_specs, check_vma=False
    )
```

time: 52.8 us -> 43.9 us (0.83)
  Pallas kernels: 48.5 us -> 43 us
  local copies, waits for them, and re-layouts: 3.53 us -> 0 us
    pallas_call x2, Pallas kernels: 48.5 us -> 43 us  [the longest x1 33.8 us: first(): pl.pallas_call(functools.partial(first_kernel, nz, nc, owned), out_shape=...]
    unnamed x6 -> x0, local copies, waits for them, and re-layouts: 2.84 us -> none
    pad x1 -> x0, local copies, waits for them, and re-layouts: 0.69 us -> none  [on_device(): jnp.pad(coarse_ids.T, ((0, 8 - coarse_ids.shape[1]), (0, 128 - per_sender...]
where the time goes in v2:
time: 43.9 us; the launch traced here: 43.8 us
  Pallas kernels  43 us (98%)
  between operations  0.8 us (2%)
    pallas_call x1, Pallas kernels, first(): pl.pallas_call(functools.partial(first_kernel, nz, nc, owned), out_shape=...  33.8 us
    pallas_call x1, Pallas kernels, second(): pl.pallas_call(second_kernel, out_shape=(jax.ShapeDtypeStruct(f1.shape, B...  9.2 us

profile of v2, /device:TPU:0, one launch (start us, length us, event | category | flops | bytes accessed | tf_op | source)
XLA Modules:
  0.0 43.8 jit_solution(17260604187082017839)
XLA Ops:
  0.6 33.8 %shard_map.68 = (bf16[2048,1024]{1,0:T(8,128)(2,1)}, bf16[512,1024]{1,0:T(8,128)(2,1)}, s32[2048,128]{1,0:T(8,128)}, s32[8,128]{1,0:T(8,128)}, f32[4,8,128]{2,1,0:T(8,128)}, /*index=5*/bf16[128,1024]{1,0:T(8,128)(2,1)}) custom-call(bf16[64,1024]{1,0:T(8,128)(2,1)} %rows_ref.1, s32[4,64]{1,0:T(4,128)} %bitcast.3, s32[256,128]{1,0:T(8,128)} %bitcast.2, ...), custom_call_target="tpu_custom_call" | custom-call | tf_op jit(solution)/shard_map/pallas_call | solution.py:420
  34.4 9.2 %shard_map.69 = (bf16[2048,1024]{1,0:T(8,128)(2,1)}, bf16[128,1024]{1,0:T(8,128)(2,1)}) custom-call(bf16[2048,1024]{1,0:T(8,128)(2,1)} %get-tuple-element.8.f1_hbm, bf16[512,1024]{1,0:T(8,128)(2,1)} %get-tuple-element.9.arrived_hbm, s32[2048,128]{1,0:T(8,128)} %get-tuple-element.10.pcol_hbm, s32[8,128]{1,0:T(8,128)} %get-tuple-element.11.scl_hbm, ...), custom_call_target="tpu_custom_call" | custom-call | tf_op jit(solution)/shard_map/pallas_call | solution.py:536

commit v3 on v2

--- a/solution.py
+++ b/solution.py
@@ -11,6 +11,20 @@
 ITERS = 2
 MOST = 4
 VMEM_LIMIT = 60 * 2**20
+FLOOR = -1e30
+
+
+def tile_softmax(l):
+    top = jnp.maximum(jnp.max(l, axis=0, keepdims=True), FLOOR)
+    e = jnp.exp2(l - top)
+    return e, top, jnp.sum(e, axis=0, keepdims=True)
+
+
+def tile_factors(tops, sums, q):
+    best = functools.reduce(jnp.maximum, tops)
+    shares = [jnp.exp2(top - best) for top in tops]
+    scale = q / sum(share * total for share, total in zip(shares, sums))
+    return [share * scale for share in shares]
 BF = jnp.bfloat16
 F32 = jnp.float32
 NT = (((1,), (1,)), ((), ()))
@@ -277,24 +291,21 @@
 
     def pair_prob(b0, b1):
         slots_g = pair_slots(b0, b1)
-        best = jnp.full((1, 256), -jnp.inf, F32)
+        tops, sums = [], []
         for part in parts:
             d = lax.dot_general(fine_ref[part, :], slots_g, NT, preferred_element_type=F32)
             l = jnp.where(
                 twice(pcol[part, :]) == cluster2, (d - twice(norms[part, :])) * scale2, -jnp.inf
             )
-            logit[part, :] = l
-            best = jnp.maximum(best, jnp.max(l, axis=0, keepdims=True))
-        denom = jnp.zeros((1, 256), F32)
-        for part in parts:
-            e = jnp.exp2(logit[part, :] - best)
-            logit[part, :] = e
-            denom = denom + jnp.sum(e, axis=0, keepdims=True)
-        return jnp.concatenate([sq_first[b0][:1], sq_first[b1][:1]], axis=1) / denom
-
-    def pair_sum(i, b0, b1, factor):
+            logit[part, :], top, total_e = tile_softmax(l)
+            tops.append(top)
+            sums.append(total_e)
+        slot_q = jnp.concatenate([sq_first[b0][:1], sq_first[b1][:1]], axis=1)
+        return tile_factors(tops, sums, slot_q)
+
+    def pair_sum(i, b0, b1, factors):
         slots_g = pair_slots(b0, b1)
-        for part in parts:
+        for part, factor in zip(parts, factors):
             resp = logit[part, :] * factor
             fsum = jnp.dot(resp.astype(BF), slots_g, preferred_element_type=F32)
             mass = resp[:, :128] + resp[:, 128:]
@@ -342,7 +353,9 @@
                 prep(order[k])
             elif k == nz // 2:
                 pair_sum(0, *pairs[0], pair_prob(*pairs[0]))
-        for k in range(nz // 2, nz):
+                wait_other(order[k])
+                prep(order[k])
+        for k in range(nz // 2 + 1, nz):
             wait_other(order[k])
             prep(order[k])
         arrived_copy()
@@ -498,7 +511,7 @@
         c.wait()
     slot_cluster = jnp.concatenate([scl_ref[:1, :]] * groups, axis=1)
     slot_q = jnp.concatenate([sq_ref[b, :1, :] for b in range(groups)], axis=1)
-    best = jnp.full((1, slots), -jnp.inf, F32)
+    tops, sums = [], []
     for part, pending in zip(parts, loads):
         for c in pending:
             c.wait()
@@ -508,17 +521,13 @@
         d = lax.dot_general(ft, arrived[...], NT, preferred_element_type=F32)
         same = jnp.concatenate([pcol[part, :]] * groups, axis=1) == slot_cluster
         l = jnp.where(same, (d - norm) * scale2, -jnp.inf)
-        logit[part, :] = l
-        best = jnp.maximum(best, jnp.max(l, axis=0, keepdims=True))
-    denom = jnp.zeros((1, slots), F32)
-    for part in parts:
-        e = jnp.exp2(logit[part, :] - best)
-        logit[part, :] = e
-        denom = denom + jnp.sum(e, axis=0, keepdims=True)
-    factor = slot_q / denom
+        logit[part, :], top, total_e = tile_softmax(l)
+        tops.append(top)
+        sums.append(total_e)
+    factors = tile_factors(tops, sums, slot_q)
     copies = [small[3]]
     for b, part in enumerate(parts):
-        resp = logit[part, :] * factor
+        resp = logit[part, :] * factors[b]
         mass = jnp.sum(resp, axis=1, keepdims=True)
         fsum = jnp.dot(resp.astype(BF), arrived[...], preferred_element_type=F32)
         result[part, :] = (

time: 43.9 us -> 43.7 us (level); the launches traced: 43.8 us -> 42.8 us
  Pallas kernels: 43 us -> 42 us
    pallas_call x1, Pallas kernels: 33.8 us -> 32.9 us  [first(): pl.pallas_call(functools.partial(first_kernel, nz, nc, owned), out_shape=...]
where the time goes in v3:
time: 43.7 us; the launch traced here: 42.8 us
  Pallas kernels  42 us (96%)
  between operations  0.8 us (2%)
    pallas_call x1, Pallas kernels, first(): pl.pallas_call(functools.partial(first_kernel, nz, nc, owned), out_shape=...  32.9 us
    pallas_call x1, Pallas kernels, second(): pl.pallas_call(second_kernel, out_shape=(jax.ShapeDtypeStruct(f1.shape, B...  9.2 us

profile of v3, /device:TPU:0, one launch (start us, length us, event | category | flops | bytes accessed | tf_op | source)
XLA Modules:
  0.0 42.8 jit_solution(4752878534664412939)
XLA Ops:
  0.6 32.9 %shard_map.68 = (bf16[2048,1024]{1,0:T(8,128)(2,1)}, bf16[512,1024]{1,0:T(8,128)(2,1)}, s32[2048,128]{1,0:T(8,128)}, s32[8,128]{1,0:T(8,128)}, f32[4,8,128]{2,1,0:T(8,128)}, /*index=5*/bf16[128,1024]{1,0:T(8,128)(2,1)}) custom-call(bf16[64,1024]{1,0:T(8,128)(2,1)} %rows_ref.1, s32[4,64]{1,0:T(4,128)} %bitcast.3, s32[256,128]{1,0:T(8,128)} %bitcast.2, ...), custom_call_target="tpu_custom_call" | custom-call | tf_op jit(solution)/shard_map/pallas_call | solution.py:433
  33.5 9.2 %shard_map.69 = (bf16[2048,1024]{1,0:T(8,128)(2,1)}, bf16[128,1024]{1,0:T(8,128)(2,1)}) custom-call(bf16[2048,1024]{1,0:T(8,128)(2,1)} %get-tuple-element.8.f1_hbm, bf16[512,1024]{1,0:T(8,128)(2,1)} %get-tuple-element.9.arrived_hbm, s32[2048,128]{1,0:T(8,128)} %get-tuple-element.10.pcol_hbm, s32[8,128]{1,0:T(8,128)} %get-tuple-element.11.scl_hbm, ...), custom_call_target="tpu_custom_call" | custom-call | tf_op jit(solution)/shard_map/pallas_call | solution.py:545
